TPU v7x, 32 devices: a whole 2x2x4 slice. The times are simulated.
32 devices in a mesh: gx: 16 (over z, x, core), gy: 2 (over y).
Axes of the slice: x: 2, y: 2, z: 4, core: 2. Of those that a mesh axis runs over, the one named last changes fastest.
Arguments:
- checkpoint: float32 [19, 128, 512], P(None, 'gx', 'gy'), as said below
- cotangent: float32 [19, 128, 512], P(None, 'gx', 'gy'), may hold values from -6 to 6
- blade_area: float32 [1536], replicated, may hold values from 0.5 to 2
- hub_tile: int32 [16], replicated, may hold values from 0 to 31
- point_side: int32 [1536], replicated, may hold values from 0 to 8
- point_local: int32 [1536], replicated, may hold values from 0 to 2047
Outputs:
- grad_checkpoint: float32 [19, 128, 512], P(None, 'gx', 'gy')
- grad_area: float32 [1536], replicated
Inputs may be any that keep to these rules, and one draw needn't show every extreme that they name: `hub_tile`: tile ids count every tile of the slab. `point_side`: every actuator point lies in its hub tile or one of the eight tiles around it. `checkpoint`: populations are positive and near a local equilibrium with density near one and streamwise velocity near 0.08.
All inputs are finite; a program needn't handle non-finite values.
Results may differ from a plain program's by a relative error of at most 0.0003.
Values sent between devices are 32-bit elements; how exact they have to be, the bound alone decides.
A program may use at most 128 MiB of HBM per device.

v0:
```python
import functools

import jax
import jax.numpy as jnp
import numpy as np
from jax import lax
from jax.experimental import pallas as pl
from jax.experimental.pallas import tpu as pltpu
from jax.sharding import PartitionSpec as P

NZ = 16
STEPS = 4
NTURB = 16
PTS = 96
LANES = 128
SUBCELLS = 4

TAU_ZERO = 0.52
SMAGORINSKY = 0.17 * 0.17
TINY = 1e-10
THRUST = 4.0
GHOST_RATES = np.array([1.05, 1.15, 1.25, 1.35, 1.45, 1.55, 1.65, 1.75, 1.85])
MESH = pl.DeviceIdType.MESH


def lattice():
    axis_part = [(1, 0, 0), (-1, 0, 0), (0, 1, 0), (0, -1, 0), (0, 0, 1), (0, 0, -1)]
    edge_part = [
        (1, 1, 0),
        (-1, -1, 0),
        (1, -1, 0),
        (-1, 1, 0),
        (1, 0, 1),
        (-1, 0, -1),
        (1, 0, -1),
        (-1, 0, 1),
        (0, 1, 1),
        (0, -1, -1),
        (0, 1, -1),
        (0, -1, 1),
    ]
    vectors = np.array([(0, 0, 0)] + axis_part + edge_part) * 1.0
    weights = np.array([1.0 / 3.0] + [1.0 / 18.0] * 6 + [1.0 / 36.0] * 12)
    opposite = np.array(
        [int(np.argmin(np.abs(vectors + vectors[column]).sum(1))) for column in range(19)]
    )
    return (vectors, weights, opposite)


def orthonormal(monomials, weights):
    rows = []
    for entry in monomials:
        vector = entry * 1.0
        for sweep in range(2):
            for other in rows:
                vector = vector - np.sum(weights * vector * other) * other
        vector = vector / np.sqrt(np.sum(weights * vector * vector))
        rows.append(vector)
    return np.stack(rows, 0)


def basis_table():
    vectors, weights, opposite = lattice()
    x, y, z = (vectors[:, 0], vectors[:, 1], vectors[:, 2])
    monomials = [np.ones(19), x, y, z, x * x, y * y, z * z, x * y, x * z, y * z]
    monomials += [x * y * y, x * z * z, y * x * x, y * z * z, z * x * x, z * y * y]
    monomials += [x * x * y * y, x * x * z * z, y * y * z * z]
    return orthonormal(monomials, weights)


VECTORS, WEIGHTS, OPPOSITE = lattice()
BASIS = basis_table()
VEC = [tuple(int(c) for c in row) for row in VECTORS]
INDEX = {vec: i for i, vec in enumerate(VEC)}
OPP = [int(i) for i in OPPOSITE]
PUSH = [float(p) for p in 3.0 * WEIGHTS * VECTORS[:, 0]]


def moving(axis, sign):
    return [i for i in range(19) if VEC[i][axis] == sign]


def total(values):
    values = list(values)
    while len(values) > 1:
        pairs = [values[k] + values[k + 1] for k in range(0, len(values) - 1, 2)]
        values = pairs + values[len(values) - len(values) % 2 :]
    return values[0]


def weighted(coefs, values):
    return total([float(c) * v for c, v in zip(coefs, values) if abs(c) > 1e-9])


def density_of(f):
    return total(f)


def momentum_of(f, axis):
    return total(f[i] for i in moving(axis, 1)) - total(f[i] for i in moving(axis, -1))


def collide(*f):
    rho = density_of(f)
    mom = [momentum_of(f, a) for a in range(3)]
    inv = 1.0 / rho
    even = {0: f[0]}
    planes = [(0, 1), (0, 2), (1, 2)]
    unit = np.eye(3, dtype=int)
    diff, cross = {}, {}
    for a in range(3):
        p = INDEX[tuple(unit[a])]
        even[a + 1] = f[p] + f[OPP[p]]
        diff[(a,)] = f[p] - f[OPP[p]]
    for k, (a, b) in enumerate(planes):
        p, q = INDEX[tuple(unit[a] + unit[b])], INDEX[tuple(unit[a] - unit[b])]
        sp, sq = f[p] + f[OPP[p]], f[q] + f[OPP[q]]
        dp, dq = f[p] - f[OPP[p]], f[q] - f[OPP[q]]
        even[4 + k] = sp + sq
        cross[k] = sp - sq
        diff[(a, b)] = dp + dq
        diff[(b, a)] = dp - dq
    stress = []
    for a in range(3):
        near = [4 + k for k, pl_ in enumerate(planes) if a in pl_]
        second = even[a + 1] + even[near[0]] + even[near[1]]
        stress.append(second - rho * (1.0 / 3.0) - mom[a] * mom[a] * inv)
    for k, (a, b) in enumerate(planes):
        stress.append(cross[k] - mom[a] * mom[b] * inv)
    square = total([p * p for p in stress[:3]]) + 2.0 * total([p * p for p in stress[3:]])
    tau = 0.5 * (
        TAU_ZERO
        + jnp.sqrt(TAU_ZERO * TAU_ZERO + 18.0 * SMAGORINSKY * jnp.sqrt(square + TINY) * inv)
    )
    rate = 1.0 / tau
    relaxed = [p * rate for p in stress]
    trace = (relaxed[0] + relaxed[1] + relaxed[2]) * (1.0 / 3.0)
    members = [0] + [INDEX[tuple(unit[a])] for a in range(3)]
    members += [INDEX[tuple(unit[a] + unit[b])] for a, b in planes]
    ghosts = [weighted(BASIS[r][members], [even[c] for c in range(7)]) for r in (16, 17, 18)]
    drop_even = []
    for c, m in enumerate(members):
        part = weighted([WEIGHTS[m] * GHOST_RATES[r - 10] * BASIS[r][m] for r in (16, 17, 18)], ghosts)
        if c == 0:
            aniso = -trace
        elif c < 4:
            aniso = relaxed[c - 1] - trace
        else:
            a, b = planes[c - 4]
            aniso = relaxed[a] + relaxed[b] - trace
        drop_even.append(part + float(4.5 * WEIGHTS[m]) * aniso)
    drop_odd = {}
    for a in range(3):
        others = [b for b in range(3) if b != a]
        kinds = [(a,)] + [(a, b) for b in others]
        reps = [INDEX[tuple(unit[a])]] + [INDEX[tuple(unit[a] + unit[b])] for b in others]
        rows = (10 + 2 * a, 11 + 2 * a)
        odd = [weighted(BASIS[r][reps], [diff[k] for k in kinds]) for r in rows]
        for kind, m in zip(kinds, reps):
            drop_odd[kind] = weighted([WEIGHTS[m] * GHOST_RATES[r - 10] * BASIS[r][m] for r in rows], odd)
    out = [None] * 19
    out[0] = f[0] - drop_even[0]
    for a in range(3):
        p = INDEX[tuple(unit[a])]
        out[p] = f[p] - (drop_even[a + 1] + drop_odd[(a,)])
        out[OPP[p]] = f[OPP[p]] - (drop_even[a + 1] - drop_odd[(a,)])
    for k, (a, b) in enumerate(planes):
        p, q = INDEX[tuple(unit[a] + unit[b])], INDEX[tuple(unit[a] - unit[b])]
        shear = 0.25 * relaxed[3 + k]
        plus, minus = drop_even[4 + k] + shear, drop_even[4 + k] - shear
        odd_p = drop_odd[(a, b)] + drop_odd[(b, a)]
        odd_q = drop_odd[(a, b)] - drop_odd[(b, a)]
        out[p] = f[p] - (plus + odd_p)
        out[OPP[p]] = f[OPP[p]] - (plus - odd_p)
        out[q] = f[q] - (minus + odd_q)
        out[OPP[q]] = f[OPP[q]] - (minus - odd_q)
    return tuple(out)


RIMS = [(1, 0, 0, 0, 2), (-1, 0, 2, 2, 2), (0, 1, 4, 4, 1), (0, -1, 5, 5, 1)]
RIMS += [(1, 1, 4, 6, 1), (1, -1, 5, 7, 1), (-1, 1, 4, 8, 1), (-1, -1, 5, 9, 1)]
CORNER = {(dx, dy): dst for dx, dy, src, dst, count in RIMS[4:]}
SIDES = [(dx, dy) for dy in (1, -1) for dx in (0, 1, -1)]
REACH = 3
HALOS = 2 * STEPS
PARTIALS = 2 * STEPS - 1


def near_offsets(size, reach):
    return sorted({d % size for d in range(-reach, reach + 1)})


def rim_copies(nx, ny):
    copies = []
    for dx, dy, src, dst, count in RIMS:
        where = (dx % nx, dy % ny)
        if copies:
            last, s, d, c = copies[-1]
            if last == where and s + c == src and d + c == dst:
                copies[-1] = (last, s, d, c + count)
                continue
        copies.append((where, src, dst, count))
    return copies


def thirds(value):
    high = value.astype(jnp.bfloat16).astype(jnp.float32)
    rest = value - high
    middle = rest.astype(jnp.bfloat16).astype(jnp.float32)
    parts = [high, middle, rest - middle, jnp.zeros_like(value)]
    return jnp.concatenate(parts, axis=0).astype(jnp.bfloat16)


def join_thirds(product):
    rows = product.shape[0] // 4
    return product[:rows] + (product[rows : 2 * rows] + product[2 * rows : 3 * rows])


def kernel(nx, ny, checkpoint, cotangent, area, cell, grad, area_grad, flats, spread, grads,
           ext_x, ext_y, halo_out, halo_in, rim_out, rim_in, part_out, part_in, sum_out, sum_a, sum_b,
           halo_sent, halo_got, rim_sent, rim_got, part_sent, part_got, sum_sent, sum_got):
    ix, iy = lax.axis_index("gx"), lax.axis_index("gy")
    near = [(dx, dy) for dx in near_offsets(nx, REACH) for dy in near_offsets(ny, REACH)]
    near = [o for o in near if o != (0, 0)]
    near.sort(key=lambda o: (-min(o[0], nx - o[0]), -min(o[1], ny - o[1])))
    low = SUBCELLS
    group = [(a, b) for a in range(low) for b in range(ny) if (a, b) != (0, 0)]
    far = list(range(1, nx // low))

    def at(dx, dy):
        return (lax.rem(ix + dx, nx), lax.rem(iy + dy, ny))

    base = lax.rem(ix, low)

    def in_group(a, b):
        return (ix - base + lax.rem(base + a, low), lax.rem(iy + b, ny))

    def in_far(c):
        return (lax.rem(ix + low * c, nx), iy)

    targets = [at(*o) for o in near] + [in_group(*o) for o in group] + [in_far(c) for c in far]
    barrier = pltpu.get_barrier_semaphore()
    for target in targets:
        pl.semaphore_signal(barrier, inc=1, device_id=target, device_id_type=MESH)

    rows, span = checkpoint.shape[1:]
    half = span - LANES
    row = lax.broadcasted_iota(jnp.int32, (rows, span), 0)
    lane = lax.broadcasted_iota(jnp.int32, (rows, span), 1)
    z = lax.bitwise_and(lane, NZ - 1)
    first_z, last_z = z == 0, z == NZ - 1
    row_h = lax.broadcasted_iota(jnp.int32, (rows, LANES), 0)
    lane_h = lax.broadcasted_iota(jnp.int32, (rows, LANES), 1)
    slot_h = lax.shift_right_logical(lane_h, 4)
    row_t = lax.broadcasted_iota(jnp.int32, (NTURB, LANES), 0)
    lane_t = lax.broadcasted_iota(jnp.int32, (NTURB, LANES), 1)

    def turned(value, shift, axis):
        shift = shift % value.shape[axis]
        return pltpu.roll(value, shift, axis) if shift else value

    def edge_of(sign):
        return rows - 1 if sign == 1 else 0

    def rim_lane(sign):
        return LANES - NZ if sign == 1 else 0

    def side_of(value, sign):
        return value[:, half:] if sign == 1 else value[:, :LANES]

    def pack_x(values, sign):
        packed = jnp.zeros((rows, span), jnp.float32)
        for k, value in enumerate(values):
            packed = jnp.where(row == k, turned(value, k - edge_of(sign), 0), packed)
        return packed

    def pack_y(values, sign):
        packed = jnp.zeros((rows, LANES), jnp.float32)
        for k, value in enumerate(values):
            moved = turned(side_of(value, sign), NZ * k - rim_lane(sign), 1)
            packed = jnp.where(slot_h == k, moved, packed)
        return packed

    def send_halo(f, fields, e):
        for sign, start in ((1, 0), (-1, 2)):
            packed = pack_x([f[i] for i in moving(0, sign)] + fields, sign)
            halo_out[e, start] = packed[:, :LANES]
            halo_out[e, start + 1] = packed[:, half:]
        for sign, start in ((1, 4), (-1, 5)):
            halo_out[e, start] = pack_y([f[i] for i in moving(1, sign)] + fields, sign)
        for where, src, dst, count in rim_copies(nx, ny):
            pltpu.make_async_remote_copy(
                src_ref=halo_out.at[e, pl.ds(src, count)],
                dst_ref=halo_in.at[e, pl.ds(dst, count)],
                send_sem=halo_sent.at[e], recv_sem=halo_got.at[e],
                device_id=at(*where), device_id_type=MESH).start()

    def receive(e, count):
        pltpu.make_async_copy(halo_in.at[e], halo_in.at[e], halo_got.at[e]).wait()
        from_x, from_y = {}, {}
        fields_x = [None] * count
        fields_y = [jnp.zeros((rows, LANES), jnp.float32)] * count
        for sign, start in ((1, 0), (-1, 2)):
            got = jnp.concatenate([halo_in[e, start], halo_in[e, start + 1]], axis=1)
            for k, i in enumerate(moving(0, sign)):
                from_x[i] = turned(got, edge_of(sign) - k, 0)
            for k in range(count):
                value = turned(got, edge_of(sign) - 5 - k, 0)
                fields_x[k] = value if sign == 1 else jnp.where(row == 0, value, fields_x[k])
        for side, (dx, dy) in enumerate(SIDES):
            got = halo_in[e, 4 if dy == 1 else 5]
            if dx:
                got = jnp.where(row_h == edge_of(dx), halo_in[e, CORNER[(dx, dy)]], got)
            for k, i in enumerate(moving(1, dy)):
                if VEC[i][0] == dx:
                    from_y[i] = turned(got, rim_lane(dy) - NZ * k, 1)
            for k in range(count):
                value = turned(got, NZ * (side - 5 - k), 1)
                fields_y[k] = jnp.where(slot_h == side, value, fields_y[k])
        return from_x, from_y, fields_x, fields_y

    def run(f, from_x, from_y):
        out = {}
        for i in f:
            dx, dy, dz = VEC[i]
            value = f[i]
            if dx:
                value = jnp.where(row == edge_of(dx), from_x[i], value)
            if dy == 1:
                edge = jnp.where(lane_h >= LANES - NZ, from_y[i], value[:, half:])
                value = jnp.concatenate([value[:, :half], edge], axis=1)
            elif dy == -1:
                edge = jnp.where(lane_h < NZ, from_y[i], value[:, :LANES])
                value = jnp.concatenate([edge, value[:, LANES:]], axis=1)
            value = turned(turned(value, dx, 0), NZ * dy + dz, 1)
            if dz:
                value = jnp.where(first_z if dz == 1 else last_z, f[OPP[i]], value)
            out[i] = value
        return out

    def pulls_of(rate):
        lines = [jnp.broadcast_to(rate[t : t + 1], (rows, LANES)) for t in range(NTURB)]
        wides = [jnp.concatenate([line] * (span // LANES), axis=1) for line in lines]
        return (total([spread[t] * wides[t] for t in range(NTURB)]),
                total([ext_x[t] * wides[t] for t in range(NTURB)]),
                total([ext_y[t] * lines[t] for t in range(NTURB)]))

    def run_added(entries, correct, fields, fields_x, fields_y, pulls):
        add = correct(fields, [p[0] for p in pulls])
        add_x = correct(fields_x, [p[1] for p in pulls])
        add_y = correct(fields_y, [p[2] for p in pulls])
        from_x = {i: add_x(i) for i in entries if VEC[i][0]}
        from_y = {}
        for side, (dx, dy) in enumerate(SIDES):
            inside = [i for i in entries if VEC[i][:2] == (dx, dy)]
            if inside:
                value = turned(add_y(inside[0]), rim_lane(dy) - NZ * side, 1)
                from_y.update({i: value for i in inside})
        return run({i: add(i) for i in entries}, from_x, from_y)

    def turbine_sums(value):
        sums = []
        for t in range(NTURB):
            prod = spread[t] * value
            sums.append(jnp.sum(prod[:, :LANES] + prod[:, half:], axis=0, keepdims=True))
        sums = jnp.sum(jnp.concatenate(sums, axis=0), axis=1, keepdims=True)
        return jnp.broadcast_to(sums, (NTURB, LANES))

    def send_partials(sums, e):
        width = LANES // (2 * len(sums))
        packed = sums[-1][8:]
        pieces = [s[h : h + 8] for s in sums for h in (0, 8)]
        for k in range(len(pieces) - 2, -1, -1):
            packed = jnp.where(lane_h < width * (k + 1), pieces[k], packed)
        part_out[e] = packed
        for k, (dx, dy) in enumerate(near):
            pltpu.make_async_remote_copy(
                src_ref=part_out.at[e], dst_ref=part_in.at[e, k],
                send_sem=part_sent.at[e], recv_sem=part_got.at[e],
                device_id=at(dx, dy), device_id_type=MESH).start()

    def take_partials(count, e):
        width = LANES // (2 * count)
        pltpu.make_async_copy(part_in.at[e], part_in.at[e], part_got.at[e]).wait()
        both = total([part_out[e]] + [part_in[e, k] for k in range(len(near))])
        pieces = []
        for k in range(2 * count):
            inside = (lane_h >= width * k) & (lane_h < width * (k + 1))
            piece, shift = jnp.where(inside, both, 0.0), width
            while shift < LANES:
                piece, shift = piece + pltpu.roll(piece, shift, 1), 2 * shift
            pieces.append(piece)
        return [jnp.concatenate(pieces[2 * k : 2 * k + 2], axis=0) / denom for k in range(count)]

    def wide(value, t):
        line = jnp.broadcast_to(value[t : t + 1], (rows, LANES))
        return jnp.concatenate([line] * (span // LANES), axis=1)

    def onehots(t):
        index = cell[t : t + 1, :]
        across = lax.shift_right_arithmetic(index, 8)
        along = lax.bitwise_and(index, 255)
        pick_x = lax.broadcasted_iota(jnp.int32, (rows, LANES), 0) == across
        pick_j = lax.broadcasted_iota(jnp.int32, (span, LANES), 0) == along
        return pick_x, jnp.where(pick_j, 1.0, 0.0).astype(jnp.bfloat16)

    def at_points(fields):
        lines = []
        for t in range(NTURB):
            pick_x, pick_j = onehots(t)
            found = join_thirds(jnp.dot(thirds(fields(t)), pick_j, preferred_element_type=jnp.float32))
            lines.append(jnp.sum(jnp.where(pick_x, found, 0.0), axis=0, keepdims=True))
        return jnp.concatenate(lines, axis=0)

    def sum_first(value, r):
        sum_out[r, 0] = value
        for k, (a, b) in enumerate(group):
            pltpu.make_async_remote_copy(
                src_ref=sum_out.at[r, 0], dst_ref=sum_a.at[r, k], send_sem=sum_sent.at[2 * r],
                recv_sem=sum_got.at[2 * r], device_id=in_group(a, b), device_id_type=MESH).start()

    def sum_second(r):
        pltpu.make_async_copy(sum_a.at[r], sum_a.at[r], sum_got.at[2 * r]).wait()
        sum_out[r, 1] = total([sum_out[r, 0]] + [sum_a[r, k] for k in range(len(group))])
        for k, c in enumerate(far):
            pltpu.make_async_remote_copy(
                src_ref=sum_out.at[r, 1], dst_ref=sum_b.at[r, k], send_sem=sum_sent.at[2 * r + 1],
                recv_sem=sum_got.at[2 * r + 1], device_id=in_far(c), device_id_type=MESH).start()

    def sum_last(r):
        pltpu.make_async_copy(sum_b.at[r], sum_b.at[r], sum_got.at[2 * r + 1]).wait()
        return total([sum_out[r, 1]] + [sum_b[r, k] for k in range(len(far))])

    field = [checkpoint[i] for i in range(19)]
    pl.semaphore_wait(barrier, len(targets))
    send_halo(field, [], 0)

    for t in range(NTURB):
        pick_x, pick_j = onehots(t)
        weight = jnp.where(pick_x, area[t : t + 1, :], 0.0)
        spread[t] = join_thirds(lax.dot_general(
            thirds(weight), pick_j, (((1,), (1,)), ((), ())), preferred_element_type=jnp.float32))
    denom = jnp.broadcast_to(jnp.sum(area[...], axis=1, keepdims=True), (NTURB, LANES))
    for h in range(2):
        mine = [spread[8 * h + k] for k in range(8)]
        for sign, start in ((1, 0), (-1, 4)):
            packed = pack_x(mine, sign)
            rim_out[start + 2 * h] = packed[:, :LANES]
            rim_out[start + 2 * h + 1] = packed[:, half:]
        for sign, start in ((1, 8), (-1, 10)):
            rim_out[start + h] = pack_y(mine, sign)
    for where, src, dst, count in rim_copies(nx, ny):
        pltpu.make_async_remote_copy(
            src_ref=rim_out.at[pl.ds(2 * src, 2 * count)],
            dst_ref=rim_in.at[pl.ds(2 * dst, 2 * count)],
            send_sem=rim_sent.at[0], recv_sem=rim_got.at[0],
            device_id=at(*where), device_id_type=MESH).start()

    def extend_spread():
        pltpu.make_async_copy(rim_in, rim_in, rim_got.at[0]).wait()
        sides = []
        for dx, dy in SIDES:
            pair = []
            for h in range(2):
                value = rim_in[(8 if dy == 1 else 10) + h]
                if dx:
                    corner = rim_in[2 * CORNER[(dx, dy)] + h]
                    value = jnp.where(row_h == edge_of(dx), corner, value)
                pair.append(value)
            sides.append(pair)
        for h in range(2):
            ups = jnp.concatenate([rim_in[2 * h], rim_in[2 * h + 1]], axis=1)
            downs = jnp.concatenate([rim_in[4 + 2 * h], rim_in[5 + 2 * h]], axis=1)
            for k in range(8):
                up, down = turned(ups, rows - 1 - k, 0), turned(downs, -k, 0)
                ext_x[8 * h + k] = jnp.where(row == rows - 1, up, jnp.where(row == 0, down, 0.0))
                packed = jnp.zeros((rows, LANES), jnp.float32)
                for side, pair in enumerate(sides):
                    moved = turned(pair[h], NZ * (side - k), 1)
                    packed = jnp.where(slot_h == side, moved, packed)
                ext_y[8 * h + k] = packed

    def forced(fields, pulls):
        force = -THRUST * fields[0] * pulls[0]
        return lambda i: PUSH[i] * force

    def speed_fixed(fields, pulls):
        speed_bar = fields[1] * pulls[0] + fields[2] * pulls[1]
        parts = {c: (float(-c) - fields[0]) * speed_bar for c in (-1, 0, 1)}
        return lambda i: parts[VEC[i][0]]

    rotors, speeds, pulls = [], [], []
    from_x, from_y, unused_x, unused_y = receive(0, 0)
    flat = run(dict(enumerate(field)), from_x, from_y)
    pushed_on = [i for i in range(19) if PUSH[i] != 0.0]
    for s in range(STEPS):
        flat = [flat[i] for i in range(19)]
        for i in range(19):
            flats[s, i] = flat[i]
        speed = momentum_of(flat, 0) / density_of(flat)
        speeds.append(speed)
        if s == STEPS - 1:
            break
        send_partials([turbine_sums(speed)], s)
        moved = collide(*flat)
        send_halo(moved, [speed], s + 1)
        if s == 0:
            extend_spread()
        from_x, from_y, fields_x, fields_y = receive(s + 1, 1)
        flat = run(dict(enumerate(moved)), from_x, from_y)
        rotors.append(take_partials(1, s)[0])
        pulls.append(pulls_of(rotors[s]))
        added = run_added(pushed_on, forced, [speed], fields_x, fields_y, [pulls[s]])
        flat.update({i: flat[i] + added[i] for i in pushed_on})

    adjoint = [cotangent[i] for i in range(19)]
    for n in range(STEPS):
        s, e = STEPS - 1 - n, STEPS + n
        flat = [flats[s, i] for i in range(19)]
        speed = speeds[s]
        force_bar = weighted(PUSH, adjoint)
        load = -THRUST * force_bar * speed
        load_sums = turbine_sums(load)
        if n == 0:
            send_partials([turbine_sums(speed), load_sums], s)
        else:
            send_partials([load_sums], s + 2 * n)
        if n == STEPS - 1:
            rotor = rotors[s]
            found = at_points(lambda t: grads[t] + wide(rotor, t) * load)
            sum_first(jnp.where(lane_t < PTS, found, load_sums), 1)
        unused, pullback = jax.vjp(collide, *flat)
        flat_bar = pullback(tuple(adjoint))
        inverse = 1.0 / density_of(flat)
        fields = [speed, inverse, -THRUST * force_bar * inverse]
        turned_bar = [flat_bar[OPP[i]] for i in range(19)]
        send_halo(turned_bar, fields, e)
        if n == 0:
            sum_first(at_points(lambda t: speeds[0] - wide(rotors[0], t)), 0)
        elif n == 1:
            sum_second(0)
        if n == STEPS - 1:
            sum_second(1)
        from_x, from_y, fields_x, fields_y = receive(e, 3)
        pushed = run(dict(enumerate(turned_bar)), from_x, from_y)
        if n == 0:
            rotor, numer_bar = take_partials(2, s)
            pulls.append(pulls_of(rotor))
        else:
            rotor = rotors[s]
            numer_bar = take_partials(1, s + 2 * n)[0]
        added = run_added(range(19), speed_fixed, fields, fields_x, fields_y, [pulls_of(numer_bar), pulls[s]])
        adjoint = [pushed[OPP[i]] + added[OPP[i]] for i in range(19)]
        if n < STEPS - 1:
            for t in range(NTURB):
                turn = wide(rotor, t)
                part = turn * load + wide(numer_bar, t) * (speed - turn)
                grads[t] = part if n == 0 else grads[t] + part

    for i in range(19):
        grad[i] = adjoint[i]
    spread_of = sum_last(0)
    sums = sum_last(1)
    numer_bar = jnp.broadcast_to(sums[:, PTS : PTS + 1], (NTURB, LANES)) / denom
    area_grad[...] = sums + numer_bar * spread_of

    for e in range(HALOS):
        pltpu.make_async_copy(halo_in.at[e], halo_in.at[e], halo_sent.at[e]).wait()
    for e in range(PARTIALS):
        pltpu.make_async_copy(part_in.at[e], part_in.at[e], part_sent.at[e]).wait()
    pltpu.make_async_copy(rim_in, rim_in, rim_sent.at[0]).wait()
    for r in range(2):
        pltpu.make_async_copy(sum_a.at[r], sum_a.at[r], sum_sent.at[2 * r]).wait()
        pltpu.make_async_copy(sum_b.at[r], sum_b.at[r], sum_sent.at[2 * r + 1]).wait()


def body(checkpoint, cotangent, blade_area, hub_tile, point_side, point_local):
    nx, ny = lax.axis_size("gx"), lax.axis_size("gy")
    ix, iy = lax.axis_index("gx"), lax.axis_index("gy")
    pops, rows, span = checkpoint.shape
    side = point_side.reshape(NTURB, PTS)
    tile_x = (hub_tile[:, None] // ny + side // 3 - 1) % nx
    tile_y = (hub_tile[:, None] % ny + side % 3 - 1) % ny
    mine = (tile_x == ix) & (tile_y == iy)
    cell = jnp.where(mine, point_local.reshape(NTURB, PTS), -1)
    pad = ((0, 0), (0, LANES - PTS))
    cell = jnp.pad(cell, pad, constant_values=-1)
    area = jnp.pad(blade_area.reshape(NTURB, PTS), pad)
    near = len(near_offsets(nx, REACH)) * len(near_offsets(ny, REACH)) - 1
    group, far = SUBCELLS * ny - 1, nx // SUBCELLS - 1
    f32, dma = jnp.float32, pltpu.SemaphoreType.DMA
    tile, vreg = (rows, span), (rows, LANES)
    shapes = [(STEPS, pops) + tile] + [(NTURB,) + tile] * 3 + [(NTURB,) + vreg]
    shapes += [(HALOS, 6) + vreg, (HALOS, 10) + vreg, (12,) + vreg, (20,) + vreg]
    shapes += [(PARTIALS,) + vreg, (PARTIALS, near) + vreg]
    shapes += [(2, 2, NTURB, LANES), (2, group, NTURB, LANES), (2, far, NTURB, LANES)]
    whole = pl.BlockSpec(memory_space=pltpu.VMEM)
    adjoint, grads = pl.pallas_call(
        functools.partial(kernel, nx, ny),
        out_shape=(jax.ShapeDtypeStruct(checkpoint.shape, f32),
                   jax.ShapeDtypeStruct((NTURB, LANES), f32)),
        in_specs=[whole] * 4,
        out_specs=(whole, whole),
        scratch_shapes=[pltpu.VMEM(shape, f32) for shape in shapes]
        + [dma((HALOS,))] * 2 + [dma((1,))] * 2 + [dma((PARTIALS,))] * 2 + [dma((4,))] * 2,
        compiler_params=pltpu.CompilerParams(
            collective_id=0, has_side_effects=True, vmem_limit_bytes=32 * 1024 * 1024),
    )(checkpoint, cotangent, area, cell)
    return adjoint, grads[:, :PTS].reshape(NTURB * PTS)


def solution(mesh):
    return jax.shard_map(
        body,
        mesh=mesh,
        in_specs=(P(None, "gx", "gy"), P(None, "gx", "gy"), P(), P(), P(), P()),
        out_specs=(P(None, "gx", "gy"), P()),
        check_vma=False,
    )
```

profile of v0, /device:TPU:0, one launch (start us, length us, event | category | flops | bytes accessed | tf_op | source)
XLA Modules:
  0.0 54.5 jit_solution(12497555295912135868)
XLA Ops:
  0.6 0.0 copy-start.2
  0.6 0.0 copy-start
  0.7 0.7 %and_select_fusion.1 = (s32[16]{0:T(128)S(1)}, s32[16]{0:T(128)S(1)}) fusion(s32[16]{0:T(128)} %param.9), kind=kLoop, calls=%fused_computation.22 | loop fusion | flops 304 | bytes 192 | tf_op jit(solution)/shard_map/jit(floor_divide)/jit(_where)/select_n | solution.py:582
  1.4 0.0 copy-done.2
  1.4 0.1 ne.64
  1.5 0.8 %reshape.47 = f32[16,96]{1,0:T(8,128)S(1)} reshape(f32[1536]{0:T(1024)} %param.8) | data formatting | bytes 12288 | tf_op jit(solution)/shard_map/reshape | solution.py:588
  2.2 0.8 %reshape.48 = s32[16,96]{1,0:T(8,128)S(1)} reshape(s32[1536]{0:T(1024)} %param.11) | data formatting | bytes 12288 | tf_op jit(solution)/shard_map/reshape | solution.py:585
  3.0 0.1 div.23
  3.1 0.1 rem.82
  3.2 0.1 fusion.9
  3.3 0.0 copy-done
  3.3 0.0 copy-start.1
  3.3 0.9 %copy-done.1 = f32[19,8,256]{2,1,0:T(8,128)S(1)} copy-done((f32[19,8,256]{2,1,0:T(8,128)S(1)}, f32[19,8,256]{2,1,0:T(8,128)}, u32[]{:S(2)}) %copy-start.1) | copy-done | bytes 155672
  4.2 48.9 %shard_map.77 = (f32[19,8,256]{2,1,0:T(8,128)S(1)}, f32[16,128]{1,0:T(8,128)S(1)}) custom-call(f32[19,8,256]{2,1,0:T(8,128)S(1)} %copy-done, f32[19,8,256]{2,1,0:T(8,128)S(1)} %copy-done.1, f32[16,128]{1,0:T(8,128)S(1)} %pad.8.area, s32[16,128]{1,0:T(8,128)S(1)} %pad.9.cell), custom_call_target="tpu_custom_call" | custom-call | tf_op jit(solution)/shard_map/pallas_call | solution.py:598
  53.1 0.7 %reshape.49 = f32[1536]{0:T(1024)} reshape(f32[16,96]{1,0:T(8,128)S(1)} %bitcast.1) | data formatting | bytes 12288 | tf_op jit(solution)/shard_map/reshape | solution.py:609
  53.8 0.7 %copy.9 = f32[19,8,256]{2,1,0:T(8,128)} copy(f32[19,8,256]{2,1,0:T(8,128)S(1)} %get-tuple-element.12) | data formatting | bytes 311296
  (4 shorter events, 0.0 us)
Async XLA Ops:
  0.6 0.7 %copy-start.2 = (s32[1536]{0:T(1024)S(1)}, s32[1536]{0:T(1024)}, u32[]{:S(2)}) copy-start(s32[1536]{0:T(1024)} %param.10) | copy-start | bytes 18436
  0.6 2.6 %copy-start = (f32[19,8,256]{2,1,0:T(8,128)S(1)}, f32[19,8,256]{2,1,0:T(8,128)}, u32[]{:S(2)}) copy-start(f32[19,8,256]{2,1,0:T(8,128)} %checkpoint.1) | copy-start | bytes 466948
  3.3 0.9 %copy-start.1 = (f32[19,8,256]{2,1,0:T(8,128)S(1)}, f32[19,8,256]{2,1,0:T(8,128)}, u32[]{:S(2)}) copy-start(f32[19,8,256]{2,1,0:T(8,128)} %cotangent.1) | copy-start | bytes 466948
where the time goes:
time: 54.8 us; the launch traced here: 54.5 us
  Pallas kernels  48.9 us (89%)
  local copies, waits for them, and re-layouts  4.03 us (7%)
  other arithmetic  0.81 us (1%)
  between operations  0.7 us (1%)
    pallas_call x1, Pallas kernels, body(): pl.pallas_call(functools.partial(kernel, nx, ny), out_shape=(jax.ShapeDty...  48.9 us
    unnamed x7, local copies, waits for them, and re-layouts  1.58 us

commit v1 on v0

--- a/solution.py
+++ b/solution.py
@@ -177,9 +177,9 @@
     return tuple(out)
 
 
-RIMS = [(1, 0, 0, 0, 2), (-1, 0, 2, 2, 2), (0, 1, 4, 4, 1), (0, -1, 5, 5, 1)]
-RIMS += [(1, 1, 4, 6, 1), (1, -1, 5, 7, 1), (-1, 1, 4, 8, 1), (-1, -1, 5, 9, 1)]
-CORNER = {(dx, dy): dst for dx, dy, src, dst, count in RIMS[4:]}
+RIMS = [(1, 0, 0, 2), (-1, 0, 2, 2), (0, 1, 4, 1), (0, -1, 5, 1)]
+CORNERS = [(1, 1, 0, 1), (1, -1, 1, 1), (-1, 1, 2, 1), (-1, -1, 3, 1)]
+CORNER = {(dx, dy): slot for dx, dy, slot, count in CORNERS}
 SIDES = [(dx, dy) for dy in (1, -1) for dx in (0, 1, -1)]
 REACH = 3
 HALOS = 2 * STEPS
@@ -190,16 +190,14 @@
     return sorted({d % size for d in range(-reach, reach + 1)})
 
 
-def rim_copies(nx, ny):
+def merged(rims, nx, ny):
     copies = []
-    for dx, dy, src, dst, count in RIMS:
+    for dx, dy, slot, count in rims:
         where = (dx % nx, dy % ny)
-        if copies:
-            last, s, d, c = copies[-1]
-            if last == where and s + c == src and d + c == dst:
-                copies[-1] = (last, s, d, c + count)
-                continue
-        copies.append((where, src, dst, count))
+        if copies and copies[-1][0] == where:
+            copies[-1] = (where, copies[-1][1], copies[-1][2] + count)
+        else:
+            copies.append((where, slot, count))
     return copies
 
 
@@ -217,8 +215,8 @@
 
 
 def kernel(nx, ny, checkpoint, cotangent, area, cell, grad, area_grad, flats, spread, grads,
-           ext_x, ext_y, halo_out, halo_in, rim_out, rim_in, part_out, part_in, sum_out, sum_a, sum_b,
-           halo_sent, halo_got, rim_sent, rim_got, part_sent, part_got, sum_sent, sum_got):
+           ext_x, ext_y, halo_out, halo_in, rim_out, rim_in, turn_out, turn_in, rim_turn_out, rim_turn_in, part_out, part_in, sum_out, sum_a, sum_b,
+           halo_sent, halo_got, rim_sent, rim_got, turn_sent, turn_got, part_sent, part_got, sum_sent, sum_got):
     ix, iy = lax.axis_index("gx"), lax.axis_index("gy")
     near = [(dx, dy) for dx in near_offsets(nx, REACH) for dy in near_offsets(ny, REACH)]
     near = [o for o in near if o != (0, 0)]
@@ -288,15 +286,23 @@
             halo_out[e, start + 1] = packed[:, half:]
         for sign, start in ((1, 4), (-1, 5)):
             halo_out[e, start] = pack_y([f[i] for i in moving(1, sign)] + fields, sign)
-        for where, src, dst, count in rim_copies(nx, ny):
-            pltpu.make_async_remote_copy(
-                src_ref=halo_out.at[e, pl.ds(src, count)],
-                dst_ref=halo_in.at[e, pl.ds(dst, count)],
-                send_sem=halo_sent.at[e], recv_sem=halo_got.at[e],
-                device_id=at(*where), device_id_type=MESH).start()
+            for dx in (1, -1):
+                edge = edge_of(dx)
+                turn_out[e, CORNER[(dx, sign)]] = halo_out[e, start, edge : edge + 1]
+        send_rims(halo_out.at[e], halo_in.at[e], turn_out.at[e], turn_in.at[e], 1,
+                  (halo_sent.at[e], halo_got.at[e], turn_sent.at[e], turn_got.at[e]))
+
+    def send_rims(out, into, turn, into_turn, scale, sems):
+        for rims, source, target, sent, got in ((RIMS, out, into) + sems[:2], (CORNERS, turn, into_turn) + sems[2:]):
+            for where, slot, count in merged(rims, nx, ny):
+                part = pl.ds(scale * slot, scale * count)
+                pltpu.make_async_remote_copy(
+                    src_ref=source.at[part], dst_ref=target.at[part], send_sem=sent, recv_sem=got,
+                    device_id=at(*where), device_id_type=MESH).start()
 
     def receive(e, count):
         pltpu.make_async_copy(halo_in.at[e], halo_in.at[e], halo_got.at[e]).wait()
+        pltpu.make_async_copy(turn_in.at[e], turn_in.at[e], turn_got.at[e]).wait()
         from_x, from_y = {}, {}
         fields_x = [None] * count
         fields_y = [jnp.zeros((rows, LANES), jnp.float32)] * count
@@ -310,7 +316,7 @@
         for side, (dx, dy) in enumerate(SIDES):
             got = halo_in[e, 4 if dy == 1 else 5]
             if dx:
-                got = jnp.where(row_h == edge_of(dx), halo_in[e, CORNER[(dx, dy)]], got)
+                got = jnp.where(row_h == edge_of(dx), turn_in[e, CORNER[(dx, dy)]], got)
             for k, i in enumerate(moving(1, dy)):
                 if VEC[i][0] == dx:
                     from_y[i] = turned(got, rim_lane(dy) - NZ * k, 1)
@@ -367,12 +373,11 @@
         return jnp.broadcast_to(sums, (NTURB, LANES))
 
     def send_partials(sums, e):
-        width = LANES // (2 * len(sums))
-        packed = sums[-1][8:]
-        pieces = [s[h : h + 8] for s in sums for h in (0, 8)]
-        for k in range(len(pieces) - 2, -1, -1):
-            packed = jnp.where(lane_h < width * (k + 1), pieces[k], packed)
-        part_out[e] = packed
+        width = LANES // (NTURB * len(sums))
+        packed = jnp.zeros((NTURB, LANES), jnp.float32)
+        for c, value in enumerate(sums):
+            packed = jnp.where(lane_t // width == row_t + NTURB * c, value, packed)
+        part_out[e] = jnp.sum(packed, axis=0, keepdims=True)
         for k, (dx, dy) in enumerate(near):
             pltpu.make_async_remote_copy(
                 src_ref=part_out.at[e], dst_ref=part_in.at[e, k],
@@ -380,17 +385,16 @@
                 device_id=at(dx, dy), device_id_type=MESH).start()
 
     def take_partials(count, e):
-        width = LANES // (2 * count)
+        width = LANES // (NTURB * count)
         pltpu.make_async_copy(part_in.at[e], part_in.at[e], part_got.at[e]).wait()
         both = total([part_out[e]] + [part_in[e, k] for k in range(len(near))])
-        pieces = []
-        for k in range(2 * count):
-            inside = (lane_h >= width * k) & (lane_h < width * (k + 1))
-            piece, shift = jnp.where(inside, both, 0.0), width
-            while shift < LANES:
-                piece, shift = piece + pltpu.roll(piece, shift, 1), 2 * shift
-            pieces.append(piece)
-        return [jnp.concatenate(pieces[2 * k : 2 * k + 2], axis=0) / denom for k in range(count)]
+        both = jnp.broadcast_to(both, (NTURB, LANES))
+        out = []
+        for c in range(count):
+            picked = jnp.where(lane_t == width * (row_t + NTURB * c), both, 0.0)
+            line = jnp.sum(picked, axis=1, keepdims=True)
+            out.append(jnp.broadcast_to(line, (NTURB, LANES)) / denom)
+        return out
 
     def wide(value, t):
         line = jnp.broadcast_to(value[t : t + 1], (rows, LANES))
@@ -449,22 +453,24 @@
             rim_out[start + 2 * h + 1] = packed[:, half:]
         for sign, start in ((1, 8), (-1, 10)):
             rim_out[start + h] = pack_y(mine, sign)
-    for where, src, dst, count in rim_copies(nx, ny):
-        pltpu.make_async_remote_copy(
-            src_ref=rim_out.at[pl.ds(2 * src, 2 * count)],
-            dst_ref=rim_in.at[pl.ds(2 * dst, 2 * count)],
-            send_sem=rim_sent.at[0], recv_sem=rim_got.at[0],
-            device_id=at(*where), device_id_type=MESH).start()
+    for sign, start in ((1, 8), (-1, 10)):
+        for dx in (1, -1):
+            for h in range(2):
+                edge = edge_of(dx)
+                rim_turn_out[2 * CORNER[(dx, sign)] + h] = rim_out[start + h, edge : edge + 1]
+    send_rims(rim_out, rim_in, rim_turn_out, rim_turn_in, 2,
+              (rim_sent.at[0], rim_got.at[0], rim_sent.at[1], rim_got.at[1]))
 
     def extend_spread():
         pltpu.make_async_copy(rim_in, rim_in, rim_got.at[0]).wait()
+        pltpu.make_async_copy(rim_turn_in, rim_turn_in, rim_got.at[1]).wait()
         sides = []
         for dx, dy in SIDES:
             pair = []
             for h in range(2):
                 value = rim_in[(8 if dy == 1 else 10) + h]
                 if dx:
-                    corner = rim_in[2 * CORNER[(dx, dy)] + h]
+                    corner = rim_turn_in[2 * CORNER[(dx, dy)] + h]
                     value = jnp.where(row_h == edge_of(dx), corner, value)
                 pair.append(value)
             sides.append(pair)
@@ -566,9 +572,11 @@
 
     for e in range(HALOS):
         pltpu.make_async_copy(halo_in.at[e], halo_in.at[e], halo_sent.at[e]).wait()
+        pltpu.make_async_copy(turn_in.at[e], turn_in.at[e], turn_sent.at[e]).wait()
     for e in range(PARTIALS):
         pltpu.make_async_copy(part_in.at[e], part_in.at[e], part_sent.at[e]).wait()
     pltpu.make_async_copy(rim_in, rim_in, rim_sent.at[0]).wait()
+    pltpu.make_async_copy(rim_turn_in, rim_turn_in, rim_sent.at[1]).wait()
     for r in range(2):
         pltpu.make_async_copy(sum_a.at[r], sum_a.at[r], sum_sent.at[2 * r]).wait()
         pltpu.make_async_copy(sum_b.at[r], sum_b.at[r], sum_sent.at[2 * r + 1]).wait()
@@ -591,8 +599,9 @@
     f32, dma = jnp.float32, pltpu.SemaphoreType.DMA
     tile, vreg = (rows, span), (rows, LANES)
     shapes = [(STEPS, pops) + tile] + [(NTURB,) + tile] * 3 + [(NTURB,) + vreg]
-    shapes += [(HALOS, 6) + vreg, (HALOS, 10) + vreg, (12,) + vreg, (20,) + vreg]
-    shapes += [(PARTIALS,) + vreg, (PARTIALS, near) + vreg]
+    shapes += [(HALOS, 6) + vreg] * 2 + [(12,) + vreg] * 2
+    shapes += [(HALOS, 4, 1, LANES)] * 2 + [(8, 1, LANES)] * 2
+    shapes += [(PARTIALS, 1, LANES), (PARTIALS, near, 1, LANES)]
     shapes += [(2, 2, NTURB, LANES), (2, group, NTURB, LANES), (2, far, NTURB, LANES)]
     whole = pl.BlockSpec(memory_space=pltpu.VMEM)
     adjoint, grads = pl.pallas_call(
@@ -602,7 +611,7 @@
         in_specs=[whole] * 4,
         out_specs=(whole, whole),
         scratch_shapes=[pltpu.VMEM(shape, f32) for shape in shapes]
-        + [dma((HALOS,))] * 2 + [dma((1,))] * 2 + [dma((PARTIALS,))] * 2 + [dma((4,))] * 2,
+        + [dma((HALOS,))] * 2 + [dma((2,))] * 2 + [dma((HALOS,))] * 2 + [dma((PARTIALS,))] * 2 + [dma((4,))] * 2,
         compiler_params=pltpu.CompilerParams(
             collective_id=0, has_side_effects=True, vmem_limit_bytes=32 * 1024 * 1024),
     )(checkpoint, cotangent, area, cell)

time: 54.8 us -> 53.5 us (0.976)
  Pallas kernels: 48.9 us -> 47.6 us
    pallas_call x1, Pallas kernels: 48.9 us -> 47.6 us  [body(): pl.pallas_call(functools.partial(kernel, nx, ny), out_shape=(jax.ShapeDty...]
where the time goes in v1:
time: 53.5 us; the launch traced here: 53.1 us
  Pallas kernels  47.6 us (89%)
  local copies, waits for them, and re-layouts  4.03 us (8%)
  other arithmetic  0.81 us (2%)
  between operations  0.7 us (1%)
    pallas_call x1, Pallas kernels, body(): pl.pallas_call(functools.partial(kernel, nx, ny), out_shape=(jax.ShapeDty...  47.6 us
    unnamed x7, local copies, waits for them, and re-layouts  1.58 us

profile of v1, /device:TPU:0, one launch (start us, length us, event | category | flops | bytes accessed | tf_op | source)
XLA Modules:
  0.0 53.1 jit_solution(14799077948260671661)
XLA Ops:
  0.6 0.0 copy-start.2
  0.6 0.0 copy-start
  0.7 0.7 %and_select_fusion.1 = (s32[16]{0:T(128)S(1)}, s32[16]{0:T(128)S(1)}) fusion(s32[16]{0:T(128)} %param.9), kind=kLoop, calls=%fused_computation.22 | loop fusion | flops 304 | bytes 192 | tf_op jit(solution)/shard_map/jit(floor_divide)/jit(_where)/select_n | solution.py:590
  1.4 0.0 copy-done.2
  1.4 0.1 ne.64
  1.5 0.8 %reshape.47 = f32[16,96]{1,0:T(8,128)S(1)} reshape(f32[1536]{0:T(1024)} %param.8) | data formatting | bytes 12288 | tf_op jit(solution)/shard_map/reshape | solution.py:596
  2.2 0.8 %reshape.48 = s32[16,96]{1,0:T(8,128)S(1)} reshape(s32[1536]{0:T(1024)} %param.11) | data formatting | bytes 12288 | tf_op jit(solution)/shard_map/reshape | solution.py:593
  3.0 0.1 div.23
  3.1 0.1 rem.82
  3.2 0.1 fusion.9
  3.3 0.0 copy-done
  3.3 0.0 copy-start.1
  3.3 0.9 %copy-done.1 = f32[19,8,256]{2,1,0:T(8,128)S(1)} copy-done((f32[19,8,256]{2,1,0:T(8,128)S(1)}, f32[19,8,256]{2,1,0:T(8,128)}, u32[]{:S(2)}) %copy-start.1) | copy-done | bytes 155672
  4.2 47.6 %shard_map.77 = (f32[19,8,256]{2,1,0:T(8,128)S(1)}, f32[16,128]{1,0:T(8,128)S(1)}) custom-call(f32[19,8,256]{2,1,0:T(8,128)S(1)} %copy-done, f32[19,8,256]{2,1,0:T(8,128)S(1)} %copy-done.1, f32[16,128]{1,0:T(8,128)S(1)} %pad.8.area, s32[16,128]{1,0:T(8,128)S(1)} %pad.9.cell), custom_call_target="tpu_custom_call" | custom-call | tf_op jit(solution)/shard_map/pallas_call | solution.py:607
  51.8 0.7 %reshape.49 = f32[1536]{0:T(1024)} reshape(f32[16,96]{1,0:T(8,128)S(1)} %bitcast.1) | data formatting | bytes 12288 | tf_op jit(solution)/shard_map/reshape | solution.py:618
  52.5 0.7 %copy.9 = f32[19,8,256]{2,1,0:T(8,128)} copy(f32[19,8,256]{2,1,0:T(8,128)S(1)} %get-tuple-element.12) | data formatting | bytes 311296
  (4 shorter events, 0.0 us)
Async XLA Ops:
  0.6 0.7 %copy-start.2 = (s32[1536]{0:T(1024)S(1)}, s32[1536]{0:T(1024)}, u32[]{:S(2)}) copy-start(s32[1536]{0:T(1024)} %param.10) | copy-start | bytes 18436
  0.6 2.6 %copy-start = (f32[19,8,256]{2,1,0:T(8,128)S(1)}, f32[19,8,256]{2,1,0:T(8,128)}, u32[]{:S(2)}) copy-start(f32[19,8,256]{2,1,0:T(8,128)} %checkpoint.1) | copy-start | bytes 466948
  3.3 0.9 %copy-start.1 = (f32[19,8,256]{2,1,0:T(8,128)S(1)}, f32[19,8,256]{2,1,0:T(8,128)}, u32[]{:S(2)}) copy-start(f32[19,8,256]{2,1,0:T(8,128)} %cotangent.1) | copy-start | bytes 466948
